TPU v7x, 512 devices: a whole 4x4x16 slice. The times are simulated.
512 devices in a mesh: dp: 32 (over y_lo, z), tensor: 16 (over y_hi, x, core).
Axes of the slice: x: 4, y: 4 (y_hi: 2, y_lo: 2; y = y_hi * 2 + y_lo), z: 16, core: 2. Of those that a mesh axis runs over, the one named last changes fastest.
Arguments:
- grad: bfloat16 [8192, 14336], P('dp', 'tensor'), may hold values from -6 to 6
- left_basis: bfloat16 [8192, 1024], P('dp', 'tensor'), may hold values from -0.0625 to 0.0625
- right_basis: float32 [14336, 896], P('tensor'), may hold values from -0.1875 to 0.1875
- moments: float32 [1024, 14336], P('dp', 'tensor'), may hold values from 0.05 to 2
Outputs:
- new_moments: float32 [1024, 14336], P('dp', 'tensor')
- update: bfloat16 [8192, 14336], P('dp', 'tensor')
All inputs are finite; a program needn't handle non-finite values.
Results may differ from a plain program's by a relative error of at most 0.0065.
Values may be sent and summed in bfloat16 or wider, within the bound.
A program may use at most 64 MiB of HBM per device.

v0:
```python
import jax
import jax.numpy as jnp
from jax import lax
from jax.sharding import PartitionSpec as P

second_decay = 0.95
moment_eps = 1e-08


def right_apply(values, right_block):
    return jnp.dot(values, right_block, precision=lax.Precision.HIGHEST)


def right_undo(values, right_block):
    return lax.dot_general(
        values, right_block, (((1,), (1,)), ((), ())), precision=lax.Precision.HIGHEST
    )


def rescale(rotated, moments):
    new_moments = second_decay * moments + (1.0 - second_decay) * rotated * rotated
    scaled = (rotated / jnp.sqrt(new_moments + moment_eps)).astype(jnp.bfloat16)
    return (new_moments, scaled)


def per_device(grad, left_basis, right_basis, moments):
    left_rows = lax.all_gather(left_basis, "tensor", axis=1, tiled=True)
    left_cols = left_rows
    rotated = lax.psum_scatter(
        right_apply(
            lax.dot_general(
                left_cols, grad, (((0,), (0,)), ((), ())), preferred_element_type=jnp.float32
            ),
            right_basis,
        ),
        "dp",
        scatter_dimension=0,
        tiled=True,
    )
    new_moments, scaled = rescale(rotated, moments)
    unrotated = right_undo(
        lax.all_gather(scaled, "dp", axis=0, tiled=True).astype(jnp.float32), right_basis
    ).astype(jnp.bfloat16)
    left_cols = left_rows
    accumulated = jnp.dot(left_cols, unrotated, preferred_element_type=jnp.float32)
    return (new_moments, accumulated.astype(jnp.bfloat16))


def solution(mesh):
    return jax.shard_map(
        per_device,
        mesh=mesh,
        in_specs=(P("dp", "tensor"), P("dp", "tensor"), P("tensor", None), P("dp", "tensor")),
        out_specs=(P("dp", "tensor"), P("dp", "tensor")),
        check_vma=False,
    )
```

profile of v0, /device:TPU:6, one launch (start us, length us, event | category | flops | bytes accessed | tf_op | source)
XLA Modules:
  0.0 338.8 jit_solution(903738514976097256)
XLA Ops:
  7.2 0.0 copy-start
  7.2 0.0 reduce-scatter.2.cloned.1.call-start
  7.2 22.3 %all_gather.6 = bf16[256,1024]{0,1:T(8,128)(2,1)S(1)} all-gather(bf16[256,64]{0,1:T(8,128)(2,1)} %param.5), channel_id=1, replica_groups=mesh['dp'=32,'tensor'=16] {'tensor'}, dimensions={1}, use_global_device_ids=true | all-gather | bytes 557056 | tf_op jit(solution)/shard_map/all_gather | solution.py:27
  29.6 0.0 copy-start.1
  29.6 0.8 copy-done.1
  30.4 1.7 fusion.10
  32.1 0.0 copy-done
  32.1 15.0 %fusion.11 = f32[1024,896]{1,0:T(8,128)} fusion(f32[1024,896]{1,0:T(8,128)S(1)} %fusion.10, f32[896,896]{1,0:T(8,128)S(1)} %copy-done), kind=kOutput, calls=%fused_computation.8 | convolution fusion | flops 9865003008 | bytes 10551296 | tf_op jit(solution)/shard_map/dot_general | solution.py:11
  47.1 0.0 copy-start.3
  47.1 0.0 reduce-scatter.2.cloned.1.call-update
  47.1 0.0 all-gather.2.cloned.1.call-start
  47.2 145.9 %reduce-scatter.2.cloned.1.call-done = f32[32,896]{1,0:T(8,128)} async-done(((f32[1024,896]{1,0:T(8,128)}), f32[32,896]{1,0:T(8,128)}) %reduce-scatter.2.cloned.1.call-update) | async-done | bytes 114704 | tf_op jit(solution)/shard_map/reduce_scatter | solution.py:29
  193.1 0.0 copy-done.3
  193.1 1.6 multiply_convert_fusion
  194.7 0.0 all-gather.2.cloned.1.call-update
  194.7 125.7 %all-gather.2.cloned.1.call-done = bf16[1024,896]{1,0:T(8,128)(2,1)} async-done(((bf16[32,896]{1,0:T(8,128)(2,1)}), bf16[1024,896]{1,0:T(8,128)(2,1)}) %all-gather.2.cloned.1.call-update) | async-done | bytes 1835024 | tf_op jit(solution)/shard_map/all_gather | solution.py:42
  320.4 0.0 copy-start.2
  320.4 8.1 %fusion.12 = bf16[1024,896]{1,0:T(8,128)(2,1)S(1)} fusion(bf16[1024,896]{1,0:T(8,128)(2,1)} %all-gather.2.cloned.1.call-done, f32[896,896]{1,0:T(8,128)S(1)} %copy-done), kind=kOutput, calls=%fused_computation.9 | convolution fusion | flops 9865003008 | bytes 6881280 | tf_op jit(solution)/shard_map/dot_general | solution.py:15
  328.5 0.0 copy-done.2
  328.5 1.5 fusion.5
  329.9 2.0 copy.6
Async XLA Ops:
  7.2 24.9 %copy-start = (f32[896,896]{1,0:T(8,128)S(1)}, f32[896,896]{1,0:T(8,128)}, u32[]{:S(2)}) copy-start(f32[896,896]{1,0:T(8,128)} %param.6) | copy-start | bytes 9633796
  7.2 185.9 %reduce-scatter.2.cloned.1.call-start = ((), (), s32[]{:S(2)}) async-start(), calls=%async_computation.1 | async-start | bytes 3784704 | tf_op jit(solution)/shard_map/reduce_scatter | solution.py:29
  29.6 0.8 copy-start.1
  47.1 146.0 %copy-start.3 = (f32[32,896]{1,0:T(8,128)S(1)}, f32[32,896]{1,0:T(8,128)}, u32[]{:S(2)}) copy-start(f32[32,896]{1,0:T(8,128)} %param.7) | copy-start | bytes 344068
  47.1 273.2 %all-gather.2.cloned.1.call-start = ((), (), s32[]{:S(2)}) async-start(), calls=%async_computation.2 | async-start | bytes 1892352 | tf_op jit(solution)/shard_map/all_gather | solution.py:42
  320.4 8.1 %copy-start.2 = (bf16[256,1024]{0,1:T(8,128)(2,1)S(1)}, bf16[256,1024]{0,1:T(8,128)(2,1)}, u32[]{:S(2)}) copy-start(bf16[256,1024]{0,1:T(8,128)(2,1)} %copy-done.1) | copy-start | bytes 1572868
Sparse Core Ops, SparseCore 0:
  47.3 145.7 reduce-scatter.1
  195.9 124.3 all-gather.1
where the time goes:
time: 339 us
  waiting for transfers between devices  272 us (80%)
  matrix products  26.3 us (8%)
  blocking collectives  22.3 us (7%)
  between operations  14.1 us (4%)
    reduce_scatter x1, waiting for transfers between devices, per_device(): lax.psum_scatter(right_apply(lax.dot_general(left_cols, grad, (((0,), (0,...  146 us
    all_gather x1, waiting for transfers between devices, per_device(): lax.all_gather(scaled, 'dp', axis=0, tiled=True).astype(jnp.float32)  126 us
    all_gather x1, blocking collectives, per_device(): left_rows = lax.all_gather(left_basis, 'tensor', axis=1, tiled=True)  22.3 us
    dot_general x1, matrix products, right_apply(): return jnp.dot(values, right_block, precision=lax.Precision.HIGHEST)  15 us
    dot_general x1, matrix products, right_undo(): lax.dot_general(values, right_block, (((1,), (1,)), ((), ())), precision=...  8.07 us
  transfers between devices with their start and end apart: 2, of which 2 were waited for; matrix products, arithmetic and copies ran while one was open for 0% of the time, Pallas kernels for 0%

commit v1 on v0

--- a/solution.py
+++ b/solution.py
@@ -25,24 +25,19 @@
 
 def per_device(grad, left_basis, right_basis, moments):
     left_rows = lax.all_gather(left_basis, "tensor", axis=1, tiled=True)
-    left_cols = left_rows
-    rotated = lax.psum_scatter(
-        right_apply(
-            lax.dot_general(
-                left_cols, grad, (((0,), (0,)), ((), ())), preferred_element_type=jnp.float32
-            ),
-            right_basis,
+    projected = lax.psum_scatter(
+        lax.dot_general(
+            left_rows, grad, (((0,), (0,)), ((), ())), preferred_element_type=jnp.float32
         ),
         "dp",
         scatter_dimension=0,
         tiled=True,
     )
+    rotated = right_apply(projected, right_basis)
     new_moments, scaled = rescale(rotated, moments)
-    unrotated = right_undo(
-        lax.all_gather(scaled, "dp", axis=0, tiled=True).astype(jnp.float32), right_basis
-    ).astype(jnp.bfloat16)
-    left_cols = left_rows
-    accumulated = jnp.dot(left_cols, unrotated, preferred_element_type=jnp.float32)
+    unrotated = right_undo(scaled.astype(jnp.float32), right_basis).astype(jnp.bfloat16)
+    gathered = lax.all_gather(unrotated, "dp", axis=0, tiled=True)
+    accumulated = jnp.dot(left_rows, gathered, preferred_element_type=jnp.float32)
     return (new_moments, accumulated.astype(jnp.bfloat16))
 
 

time: 339 us -> 322 us (0.950)
  matrix products: 26.3 us -> 11.5 us
    dot_general x1, matrix products: 15 us -> 2.59 us  [right_apply(): return jnp.dot(values, right_block, precision=lax.Precision.HIGHEST)]
    dot_general x1, matrix products: 8.07 us -> 2.32 us  [right_undo(): lax.dot_general(values, right_block, (((1,), (1,)), ((), ())), precision=...]
    dot_general x2, matrix products: 3.18 us -> 6.63 us  [the longest x1 3.54 us: per_device(): lax.dot_general(left_rows, grad, (((0,), (0,)), ((), ())), preferred_elem...]
where the time goes in v1:
time: 322 us; the launch traced here: 321 us
  waiting for transfers between devices  270 us (84%)
  blocking collectives  22.3 us (7%)
  between operations  14.1 us (4%)
  matrix products  11.5 us (4%)
    reduce_scatter x1, waiting for transfers between devices, per_device(): lax.psum_scatter(lax.dot_general(left_rows, grad, (((0,), (0,)), ((), ())...  146 us
    all_gather x1, waiting for transfers between devices, per_device(): gathered = lax.all_gather(unrotated, 'dp', axis=0, tiled=True)  124 us
    all_gather x1, blocking collectives, per_device(): left_rows = lax.all_gather(left_basis, 'tensor', axis=1, tiled=True)  22.3 us
  transfers between devices with their start and end apart: 2, of which 2 were waited for; matrix products, arithmetic and copies ran while one was open for 0% of the time, Pallas kernels for 0%

profile of v1, /device:TPU:6, one launch (start us, length us, event | category | flops | bytes accessed | tf_op | source)
XLA Modules:
  0.0 321.2 jit_solution(15933984154885629613)
XLA Ops:
  7.2 0.0 copy-start
  7.2 0.0 reduce-scatter.2.cloned.1.call-start
  7.2 22.3 %all_gather.6 = bf16[256,1024]{0,1:T(8,128)(2,1)S(1)} all-gather(bf16[256,64]{0,1:T(8,128)(2,1)} %param.5), channel_id=1, replica_groups=mesh['dp'=32,'tensor'=16] {'tensor'}, dimensions={1}, use_global_device_ids=true | all-gather | bytes 557056 | tf_op jit(solution)/shard_map/all_gather | solution.py:27
  29.6 0.0 copy-start.1
  29.6 0.8 copy-done.1
  30.4 0.0 copy-start.3
  30.4 3.5 %fusion.4 = f32[1024,896]{1,0:T(8,128)} fusion(bf16[256,1024]{0,1:T(8,128)(2,1)S(1)} %all_gather.6, bf16[256,896]{1,0:T(8,128)(2,1)} %param.4), kind=kOutput, calls=%fused_computation.8 | convolution fusion | flops 469762048 | bytes 4653056 | tf_op jit(solution)/shard_map/dot_general | solution.py:29
  33.9 0.0 reduce-scatter.2.cloned.1.call-update
  33.9 0.0 all-gather.2.cloned.1.call-start
  34.0 145.9 %reduce-scatter.2.cloned.1.call-done = f32[32,896]{1,0:T(8,128)} async-done(((f32[1024,896]{1,0:T(8,128)}), f32[32,896]{1,0:T(8,128)}) %reduce-scatter.2.cloned.1.call-update) | async-done | bytes 114704 | tf_op jit(solution)/shard_map/reduce_scatter | solution.py:28
  179.9 0.0 copy-done
  179.9 0.0 copy-done.3
  179.9 2.6 fusion.1
  182.5 0.0 copy-start.2
  182.5 2.3 convolution_convert_fusion.1
  184.8 0.0 all-gather.2.cloned.1.call-update
  184.9 124.5 %all-gather.2.cloned.1.call-done = bf16[1024,896]{1,0:T(8,128)(2,1)} async-done(((bf16[32,896]{1,0:T(8,128)(2,1)}), bf16[1024,896]{1,0:T(8,128)(2,1)}) %all-gather.2.cloned.1.call-update) | async-done | bytes 1835024 | tf_op jit(solution)/shard_map/all_gather | solution.py:39
  309.3 3.1 fusion
  312.4 0.0 copy-done.2
  312.4 2.0 copy.6
Async XLA Ops:
  7.2 172.7 %copy-start = (f32[896,896]{1,0:T(8,128)S(1)}, f32[896,896]{1,0:T(8,128)}, u32[]{:S(2)}) copy-start(f32[896,896]{1,0:T(8,128)} %param.6) | copy-start | bytes 9633796
  7.2 172.7 %reduce-scatter.2.cloned.1.call-start = ((), (), s32[]{:S(2)}) async-start(), calls=%async_computation.1 | async-start | bytes 3784704 | tf_op jit(solution)/shard_map/reduce_scatter | solution.py:28
  29.6 0.8 copy-start.1
  30.4 149.5 %copy-start.3 = (f32[32,896]{1,0:T(8,128)S(1)}, f32[32,896]{1,0:T(8,128)}, u32[]{:S(2)}) copy-start(f32[32,896]{1,0:T(8,128)} %param.7) | copy-start | bytes 344068
  33.9 275.4 %all-gather.2.cloned.1.call-start = ((), (), s32[]{:S(2)}) async-start(), calls=%async_computation.2 | async-start | bytes 1892352 | tf_op jit(solution)/shard_map/all_gather | solution.py:39
  182.5 129.9 %copy-start.2 = (f32[32,896]{1,0:T(8,128)}, f32[32,896]{1,0:T(8,128)S(1)}, u32[]{:S(2)}) copy-start(f32[32,896]{1,0:T(8,128)S(1)} %get-tuple-element.4) | copy-start | bytes 344068
Sparse Core Ops, SparseCore 0:
  34.0 145.8 reduce-scatter.1
  185.0 124.3 all-gather.1

commit v2 on v1

v2 whole, which is shorter than its diff:
```python
import functools

import jax
import jax.numpy as jnp
from jax import lax
from jax.experimental import pallas as pl
from jax.experimental.pallas import tpu as pltpu
from jax.sharding import PartitionSpec as P

second_decay = 0.95
moment_eps = 1e-08

MESH = pl.DeviceIdType.MESH
Z, X = 16, 4
ROWS, COLS, OWN, SHARD = 256, 896, 32, 64
HALF = Z * OWN
JS = 2 * X
SPANS = ((0, 256), (256, 256), (512, 384))
NC = len(SPANS)
HOPS = tuple((8, 7) if c % 2 == 0 else (7, 8) for c in range(NC))


def split_bf16(values):
    high = values.astype(jnp.bfloat16)
    return high, (values - high.astype(jnp.float32)).astype(jnp.bfloat16)


def dot(a, b, ca, cb):
    return lax.dot_general(a, b, (((ca,), (cb,)), ((), ())), preferred_element_type=jnp.float32)


def kernel(grad, left, right, moments, new_moments, update, *scratch):
    (mine, shards, other, lrow, rows, w32, whi, wlo, mom, proj, rot) = scratch[:11]
    first, slots, gathered = (scratch[11 + NC * i : 11 + NC * (i + 1)] for i in range(3))
    (loc_s, l1_s, l1_r, lx_s, lx_r, lc_s, lc_r, g_s, g_r, o_s, o_r, rs_s, rs_r, y_s, y_r, ag_s, ag_r) = scratch[
        11 + 3 * NC :
    ]
    dp, t = lax.axis_index("dp"), lax.axis_index("tensor")
    ylo, z = dp // Z, dp % Z
    yhi, j = t // JS, t % JS
    x, core = j // 2, j % 2
    plane = ylo * Z
    up = (plane + (z + 1) % Z, t)
    down = (plane + (z + Z - 1) % Z, t)
    partner = ((1 - ylo) * Z + z, t)
    across = (dp, (1 - yhi) * JS + j)
    diagonal = ((1 - ylo) * Z + z, (1 - yhi) * JS + j)
    sibling = (dp, yhi * JS + x * 2 + (1 - core))
    xs = [(dp, yhi * JS + ((x + d) % X) * 2 + core) for d in range(1, X)]

    def remote(src, dst, ssem, rsem, dev):
        return pltpu.make_async_remote_copy(
            src_ref=src, dst_ref=dst, send_sem=ssem, recv_sem=rsem, device_id=dev, device_id_type=MESH
        )

    barrier = pltpu.get_barrier_semaphore()
    everyone = [up, down, partner, across, diagonal, sibling] + xs
    for dev in everyone:
        pl.semaphore_signal(barrier, inc=1, device_id=dev, device_id_type=MESH)
    loads = [
        pltpu.make_async_copy(grad, rows.at[ylo], loc_s.at[0]),
        pltpu.make_async_copy(right, w32, loc_s.at[1]),
        pltpu.make_async_copy(moments, mom, loc_s.at[2]),
    ]
    for load in loads:
        load.start()
    mine[...] = left[...].T
    pl.semaphore_wait(barrier, len(everyone))

    at_home = ylo == yhi
    here = shards.at[ylo, j]

    @pl.when(at_home)
    def _():
        remote(mine, here, l1_s.at[0], l1_r.at[ylo], across).start()
        shards[ylo, j] = mine[...]

    @pl.when(jnp.logical_not(at_home))
    def _():
        remote(mine, here, l1_s.at[0], l1_r.at[ylo], partner).start()
        remote(mine, here, l1_s.at[1], l1_r.at[ylo], diagonal).start()

    def grad_part(c):
        lo, n = SPANS[c]
        return remote(
            grad.at[:, pl.ds(lo, n)], rows.at[ylo, :, pl.ds(lo, n)], g_s.at[c], g_r.at[c], partner
        )

    for c in range(NC):
        grad_part(c).start()

    def to_x(r, d):
        return remote(shards.at[r, j], shards.at[r, j], lx_s.at[r, d], lx_r.at[r, d], xs[d])

    def from_x(r, d):
        jj = ((x + X - 1 - d) % X) * 2 + core
        return remote(shards.at[r, jj], shards.at[r, jj], lx_s.at[r, d], lx_r.at[r, d], xs[d])

    def to_core(r, d):
        jj = ((x + X - d) % X) * 2 + core
        return remote(shards.at[r, jj], shards.at[r, jj], lc_s.at[r, d], lc_r.at[r, d], sibling)

    def from_core(r, d):
        jj = ((x + X - d) % X) * 2 + (1 - core)
        return remote(shards.at[r, jj], shards.at[r, jj], lc_s.at[r, d], lc_r.at[r, d], sibling)

    for r in range(2):

        @pl.when(jnp.logical_not(jnp.logical_and(at_home, ylo == r)))
        def _():
            remote(mine, shards.at[r, j], l1_s.at[0], l1_r.at[r], across).wait_recv()

        for d in range(X - 1):
            to_x(r, d).start()
        to_core(r, 0).start()

    loads[1].wait()
    for lo in range(0, COLS, 128):
        high, low = split_bf16(w32[pl.ds(lo, 128), :])
        whi[pl.ds(lo, 128), :] = high
        wlo[pl.ds(lo, 128), :] = low

    for r in range(2):
        for d in range(X - 1):
            from_x(r, d).wait_recv()
            to_core(r, d + 1).start()
    for r in range(2):
        for d in range(X):
            from_core(r, d).wait_recv()
    loads[0].wait()

    def rs(c, way, s):
        hops = HOPS[c]
        src = first[c].at[way] if s == 0 else slots[c].at[way, s - 1]
        return remote(src, slots[c].at[way, s], rs_s.at[c, way, s], rs_r.at[c, way, s], (up, down)[way])

    def part(c, d):
        lo, n = SPANS[c]
        return proj[pl.ds(pl.multiple_of(d * OWN, OWN), OWN), pl.ds(lo, n)]

    def bound_for(c, way, s):
        return (z + HOPS[c][0] - s) % Z if way == 0 else (z + Z - HOPS[c][1] + s) % Z

    for c, (lo, n) in enumerate(SPANS):
        grad_part(c).wait_recv()
        total = dot(shards[0].reshape(HALF, ROWS), rows[0, :, pl.ds(lo, n)], 1, 0)
        total += dot(shards[1].reshape(HALF, ROWS), rows[1, :, pl.ds(lo, n)], 1, 0)
        proj[:, pl.ds(lo, n)] = total
        for way in range(2):
            first[c][way] = part(c, bound_for(c, way, 0)).astype(jnp.bfloat16)
            rs(c, way, 0).start()

    def to_partner():
        return remote(shards.at[1 - ylo], other, o_s, o_r, partner)

    to_partner().start()
    for s in range(1, 8):
        for c in range(NC):
            for way in range(2):
                if s < HOPS[c][way]:
                    rs(c, way, s - 1).wait_recv()
                    held = slots[c].at[way, s - 1]
                    held[...] = (held[...].astype(jnp.float32) + part(c, bound_for(c, way, s))).astype(jnp.bfloat16)
                    rs(c, way, s).start()
        if s == 2:
            lrow[ylo] = shards[ylo].reshape(HALF, ROWS).T
        if s == 5:
            to_partner().wait_recv()
            lrow[1 - ylo] = other[...].reshape(HALF, ROWS).T

    loads[2].wait()
    for c, (lo, n) in enumerate(SPANS):
        own = part(c, z)
        for way in range(2):
            last = HOPS[c][way] - 1
            rs(c, way, last).wait_recv()
            own += slots[c][way, last].astype(jnp.float32)
        high, low = split_bf16(own)
        both = dot(jnp.concatenate([high, low], axis=0), whi[pl.ds(lo, n), :], 1, 0)
        term = both[:OWN] + both[OWN:] + dot(high, wlo[pl.ds(lo, n), :], 1, 0)
        if c == 0:
            rot[...] = term
        else:
            rot[...] += term
    rotated = rot[...]
    moved = second_decay * mom[...] + (1.0 - second_decay) * rotated * rotated
    new_moments[...] = moved
    scaled = (rotated / jnp.sqrt(moved + moment_eps)).astype(jnp.bfloat16)

    def y_part(c):
        ref = gathered[c].at[ylo, z]
        return remote(ref, ref, y_s.at[c], y_r.at[c], partner)

    def ag(c, way, s):
        o = (z + Z - s) % Z if way == 0 else (z + s) % Z
        ref = gathered[c].at[:, o]
        return remote(ref, ref, ag_s.at[c, way, s], ag_r.at[c, way, s], (up, down)[way])

    def ag_in(c, way, s):
        o = (z + Z - 1 - s) % Z if way == 0 else (z + 1 + s) % Z
        ref = gathered[c].at[:, o]
        return remote(ref, ref, ag_s.at[c, way, s], ag_r.at[c, way, s], (up, down)[way])

    for c, (lo, n) in enumerate(SPANS):
        back = dot(scaled, whi[pl.ds(lo, n), :], 1, 1) + dot(scaled, wlo[pl.ds(lo, n), :], 1, 1)
        gathered[c][ylo, z] = back.astype(jnp.bfloat16)
        y_part(c).start()
    for c in range(NC):
        ref = gathered[c].at[1 - ylo, z]
        remote(ref, ref, y_s.at[c], y_r.at[c], partner).wait_recv()
        for way in range(2):
            ag(c, way, 0).start()
    for s in range(1, 8):
        for c in range(NC):
            for way in range(2):
                if s < HOPS[c][way]:
                    ag_in(c, way, s - 1).wait_recv()
                    ag(c, way, s).start()
    for c, (lo, n) in enumerate(SPANS):
        for way in range(2):
            ag_in(c, way, HOPS[c][way] - 1).wait_recv()
        total = dot(lrow[0], gathered[c][0].reshape(HALF, n), 1, 0)
        total += dot(lrow[1], gathered[c][1].reshape(HALF, n), 1, 0)
        update[:, pl.ds(lo, n)] = total.astype(jnp.bfloat16)

    remote(mine, here, l1_s.at[0], l1_r.at[0], across).wait_send()

    @pl.when(jnp.logical_not(at_home))
    def _():
        remote(mine, here, l1_s.at[1], l1_r.at[0], diagonal).wait_send()

    for r in range(2):
        for d in range(X - 1):
            to_x(r, d).wait_send()
        for d in range(X):
            to_core(r, d).wait_send()
    to_partner().wait_send()
    for c in range(NC):
        grad_part(c).wait_send()
        y_part(c).wait_send()
        for way in range(2):
            for s in range(HOPS[c][way]):
                rs(c, way, s).wait_send()
                ag(c, way, s).wait_send()


def per_device(grad, left_basis, right_basis, moments):
    bf16, f32 = jnp.bfloat16, jnp.float32
    dma = pltpu.SemaphoreType.DMA
    vmem = pl.BlockSpec(memory_space=pltpu.VMEM)
    hbm = pl.BlockSpec(memory_space=pl.ANY)
    scratch = [
        pltpu.VMEM((SHARD, ROWS), bf16),
        pltpu.VMEM((2, JS, SHARD, ROWS), bf16),
        pltpu.VMEM((JS, SHARD, ROWS), bf16),
        pltpu.VMEM((2, ROWS, HALF), bf16),
        pltpu.VMEM((2, ROWS, COLS), bf16),
        pltpu.VMEM((COLS, COLS), f32),
        pltpu.VMEM((COLS, COLS), bf16),
        pltpu.VMEM((COLS, COLS), bf16),
        pltpu.VMEM((OWN, COLS), f32),
        pltpu.VMEM((HALF, COLS), f32),
        pltpu.VMEM((OWN, COLS), f32),
    ]
    scratch += [pltpu.VMEM((2, OWN, n), bf16) for _, n in SPANS]
    scratch += [pltpu.VMEM((2, 8, OWN, n), bf16) for _, n in SPANS]
    scratch += [pltpu.VMEM((2, Z, OWN, n), bf16) for _, n in SPANS]
    scratch += [dma((3,)), dma((2,)), dma((2,)), dma((2, 3)), dma((2, 3)), dma((2, 4)), dma((2, 4))]
    scratch += [dma((NC,)), dma((NC,)), dma, dma, dma((NC, 2, 8)), dma((NC, 2, 8))]
    scratch += [dma((NC,)), dma((NC,)), dma((NC, 2, 8)), dma((NC, 2, 8))]
    return pl.pallas_call(
        kernel,
        out_shape=(
            jax.ShapeDtypeStruct((OWN, COLS), f32),
            jax.ShapeDtypeStruct((ROWS, COLS), bf16),
        ),
        in_specs=[hbm, vmem, hbm, hbm],
        out_specs=(vmem, vmem),
        scratch_shapes=scratch,
        compiler_params=pltpu.CompilerParams(
            collective_id=0, has_side_effects=True, vmem_limit_bytes=48 * 2**20
        ),
    )(grad, left_basis, right_basis, moments)


def solution(mesh):
    return jax.shard_map(
        per_device,
        mesh=mesh,
        in_specs=(P("dp", "tensor"), P("dp", "tensor"), P("tensor", None), P("dp", "tensor")),
        out_specs=(P("dp", "tensor"), P("dp", "tensor")),
        check_vma=False,
    )
```

time: 322 us -> 90.8 us (0.28)
  waiting for transfers between devices: 270 us -> 0 us
  Pallas kernels: 0 us -> 83.3 us
  blocking collectives: 22.3 us -> 0 us
  between operations: 14.1 us -> 0.65 us
  matrix products: 11.5 us -> 0 us
  local copies, waits for them, and re-layouts: 2.8 us -> 6.11 us
    reduce_scatter x1 -> x0, waiting for transfers between devices: 146 us -> none  [per_device(): lax.psum_scatter(lax.dot_general(left_rows, grad, (((0,), (0,)), ((), ())...]
    all_gather x1 -> x0, waiting for transfers between devices: 124 us -> none  [per_device(): gathered = lax.all_gather(unrotated, 'dp', axis=0, tiled=True)]
    pallas_call x0 -> x1, Pallas kernels: none -> 83.3 us  [per_device(): pl.pallas_call(kernel, out_shape=(jax.ShapeDtypeStruct((OWN, COLS), f32),...]
    all_gather x1 -> x0, blocking collectives: 22.3 us -> none  [per_device(): left_rows = lax.all_gather(left_basis, 'tensor', axis=1, tiled=True)]
    dot_general x4 -> x0, matrix products: 11.5 us -> none  [the longest x1 3.54 us: per_device(): lax.dot_general(left_rows, grad, (((0,), (0,)), ((), ())), preferred_elem...]
    unnamed x9, local copies, waits for them, and re-layouts: 2.8 us -> 6.11 us
  transfers between devices with their start and end apart: 2 -> 0, of which waited for: 2 -> 0; matrix products, arithmetic and copies ran while one was open for 0% -> 0% of each run, Pallas kernels for 0% -> 0%
where the time goes in v2:
time: 90.8 us; the launch traced here: 90.1 us
  Pallas kernels  83.3 us (92%)
  local copies, waits for them, and re-layouts  6.11 us (7%)
    pallas_call x1, Pallas kernels, per_device(): pl.pallas_call(kernel, out_shape=(jax.ShapeDtypeStruct((OWN, COLS), f32),...  83.3 us
    unnamed x9, local copies, waits for them, and re-layouts  6.11 us

profile of v2, /device:TPU:6, one launch (start us, length us, event | category | flops | bytes accessed | tf_op | source)
XLA Modules:
  0.0 90.1 jit_solution(3103259954073423401)
XLA Ops:
  0.6 0.9 copy.6.left
  1.5 0.0 copy-start
  1.5 1.9 %copy-done = f32[896,896]{1,0:T(8,128)S(1)} copy-done((f32[896,896]{1,0:T(8,128)S(1)}, f32[896,896]{1,0:T(8,128)}, u32[]{:S(2)}) %copy-start) | copy-done | bytes 3211288
  3.4 0.0 copy-start.1
  3.4 1.0 %copy-done.1 = bf16[256,896]{1,0:T(8,128)(2,1)S(1)} copy-done((bf16[256,896]{1,0:T(8,128)(2,1)S(1)}, bf16[256,896]{1,0:T(8,128)(2,1)}, u32[]{:S(2)}) %copy-start.1) | copy-done | bytes 458776
  4.4 0.0 copy-start.2
  4.4 0.9 copy-done.2
  5.3 83.3 %shard_map.59 = (f32[32,896]{1,0:T(8,128)S(1)}, bf16[256,896]{1,0:T(8,128)(2,1)S(1)}) custom-call(bf16[256,896]{1,0:T(8,128)(2,1)S(1)} %copy-done.1, bf16[256,64]{1,0:T(8,128)(2,1)S(1)} %copy.6.left, f32[896,896]{1,0:T(8,128)S(1)} %copy-done, f32[32,896]{1,0:T(8,128)S(1)} %copy-done.2), custom_call_target="tpu_custom_call" | custom-call | tf_op jit(solution)/shard_map/pallas_call | solution.py:271
  88.6 0.6 copy.9
  89.3 0.8 copy.10
Async XLA Ops:
  1.5 1.9 %copy-start = (f32[896,896]{1,0:T(8,128)S(1)}, f32[896,896]{1,0:T(8,128)}, u32[]{:S(2)}) copy-start(f32[896,896]{1,0:T(8,128)} %right.1) | copy-start | bytes 9633796
  3.4 1.0 %copy-start.1 = (bf16[256,896]{1,0:T(8,128)(2,1)S(1)}, bf16[256,896]{1,0:T(8,128)(2,1)}, u32[]{:S(2)}) copy-start(bf16[256,896]{1,0:T(8,128)(2,1)} %grad.1) | copy-start | bytes 1376260
  4.4 0.9 copy-start.2

commit v3 on v1

v3 whole, which is shorter than its diff:
```python
import jax
import jax.numpy as jnp
from jax import lax
from jax.experimental import pallas as pl
from jax.experimental.pallas import tpu as pltpu
from jax.sharding import PartitionSpec as P

second_decay = 0.95
moment_eps = 1e-08

MESH = pl.DeviceIdType.MESH
Z, X = 16, 4
ROWS, COLS, OWN, SHARD = 256, 896, 32, 64
HALF = Z * OWN
JS = 2 * X
SPANS = ((0, 256), (256, 256), (512, 256), (768, 128))
PART = OWN // 2
GPARTS = 4


def split_bf16(values):
    high = values.astype(jnp.bfloat16)
    return high, (values - high.astype(jnp.float32)).astype(jnp.bfloat16)


def dot(a, b, ca, cb):
    return lax.dot_general(a, b, (((ca,), (cb,)), ((), ())), preferred_element_type=jnp.float32)


def kernel(grad, left, right, moments, new_moments, update, *scratch):
    (shards, other, lrow, rows, w32, whi, wlo, mom, proj, leaving, slots, gathered, total) = scratch[:13]
    (loc_s, l_s, l_r, lx_s, lx_r, lc_s, lc_r, g_s, g_r, o_s, o_r, rs_s, rc_r, rl_r, ag_s, ac_r, al_r, y_s, y_r) = (
        scratch[13:]
    )
    dp, t = lax.axis_index("dp"), lax.axis_index("tensor")
    ylo, z = dp // Z, dp % Z
    yhi, j = t // JS, t % JS
    x, core = j // 2, j % 2

    def along(step):
        return (ylo * Z + (z + Z + step) % Z, t)

    near, far = (along(1), along(-1)), (along(2), along(-2))
    partner = ((1 - ylo) * Z + z, t)
    across = (dp, (1 - yhi) * JS + j)
    diagonal = ((1 - ylo) * Z + z, (1 - yhi) * JS + j)
    sibling = (dp, yhi * JS + x * 2 + (1 - core))
    xs = [(dp, yhi * JS + ((x + d) % X) * 2 + core) for d in range(1, X)]

    def remote(src, dst, ssem, rsem, dev):
        return pltpu.make_async_remote_copy(
            src_ref=src, dst_ref=dst, send_sem=ssem, recv_sem=rsem, device_id=dev, device_id_type=MESH
        )

    barrier = pltpu.get_barrier_semaphore()
    everyone = [*near, *far, partner, across, diagonal, sibling] + xs
    for dev in everyone:
        pl.semaphore_signal(barrier, inc=1, device_id=dev, device_id_type=MESH)
    here = shards.at[ylo, core, x]
    loads = [
        pltpu.make_async_copy(grad, rows.at[ylo], loc_s.at[0]),
        pltpu.make_async_copy(right, w32, loc_s.at[1]),
        pltpu.make_async_copy(moments, mom, loc_s.at[2]),
    ]
    keep = pltpu.make_async_copy(left, here, loc_s.at[3])
    at_home = ylo == yhi
    away = jnp.logical_not(at_home)
    pl.when(at_home)(keep.start)
    for load in loads:
        load.start()
    pl.semaphore_wait(barrier, len(everyone))

    to_across = remote(left, here, l_s.at[0], l_r.at[ylo], across)
    to_mate = remote(left, here, l_s.at[0], l_r.at[ylo], partner)
    to_diagonal = remote(left, here, l_s.at[1], l_r.at[ylo], diagonal)
    pl.when(at_home)(to_across.start)
    pl.when(away)(to_mate.start)
    pl.when(away)(to_diagonal.start)

    def grad_part(p):
        cut = pl.ds(p * (ROWS // GPARTS), ROWS // GPARTS)
        return remote(grad.at[cut], rows.at[ylo, cut], g_s, g_r, partner)

    for p in range(GPARTS):
        grad_part(p).start()

    def to_x(r, d):
        ref = shards.at[r, core, x]
        return remote(ref, ref, lx_s.at[r, d - 1], lx_r.at[r, d - 1], xs[d - 1])

    def from_x(r, d):
        ref = shards.at[r, core, (x + X - d) % X]
        return remote(ref, ref, lx_s.at[r, d - 1], lx_r.at[r, d - 1], xs[d - 1])

    def to_core(r):
        ref = shards.at[r, core]
        return remote(ref, ref, lc_s.at[r], lc_r.at[r], sibling)

    def from_core(r):
        ref = shards.at[r, 1 - core]
        return remote(ref, ref, lc_s.at[r], lc_r.at[r], sibling)

    for k in range(2):
        r = (ylo + k) % 2
        arrived = remote(left, shards.at[r, core, x], l_s.at[0], l_r.at[r], sibling).wait_recv
        if k == 0:
            pl.when(at_home)(keep.wait)
            pl.when(away)(arrived)
        else:
            arrived()
        for d in range(1, X):
            to_x(r, d).start()

    loads[1].wait()
    for lo in range(0, COLS, 128):
        high, low = split_bf16(w32[pl.ds(lo, 128), :])
        whi[pl.ds(lo, 128), :] = high
        wlo[pl.ds(lo, 128), :] = low

    for k in range(2):
        r = (ylo + k) % 2
        for d in range(1, X):
            from_x(r, d).wait_recv()
        to_core(r).start()

    def project(c):
        for lo, n in SPANS:
            part = dot(shards[0, c].reshape(X * SHARD, ROWS), rows[0, :, pl.ds(lo, n)], 1, 0)
            part += dot(shards[1, c].reshape(X * SHARD, ROWS), rows[1, :, pl.ds(lo, n)], 1, 0)
            proj[pl.ds(pl.multiple_of(c * X * SHARD, X * SHARD), X * SHARD), pl.ds(lo, n)] = part

    loads[0].wait()
    remote(grad, rows.at[1 - ylo], g_s, g_r, partner).wait_recv()
    project(core)
    for r in range(2):
        from_core(r).wait_recv()
    project(1 - core)

    def chunk(d, p=None):
        d = (d + Z) % Z
        row = ((d // 2) % 2) * (X * SHARD) + (d // 4) * SHARD + (d % 2) * OWN
        if p is None:
            return proj[pl.ds(pl.multiple_of(row, OWN), OWN), :]
        return proj[pl.ds(pl.multiple_of(row + p * PART, PART), PART), :]

    def half(ref, p):
        return ref.at[pl.ds(p * PART, PART)]

    def chain_in(way, k):
        return slots.at[4 * way + k]

    def leaf_in(way, k):
        return slots.at[7 + 4 * way + k]

    def chain_source(way, k):
        if way == 0:
            return leaving.at[0] if k == 0 else chain_in(0, k - 1)
        return leaf_in(1, k)

    def rs_chain(way, k, p):
        return remote(
            half(chain_source(way, k), p), half(chain_in(way, k), p), rs_s, rc_r.at[way, k, p], far[way]
        )

    def rs_leaf(way, k):
        return remote(leaving.at[1 + 4 * way + k], leaf_in(way, k), rs_s, rl_r.at[way, k], near[way])

    def send_leaf(way, k):
        leaving[1 + 4 * way + k] = chunk(z + 7 - 2 * k if way == 0 else z - 7 + 2 * k).astype(jnp.bfloat16)
        rs_leaf(way, k).start()

    def send_chain(way, k):
        first = way == 0 and k == 0
        if not first:
            rs_leaf(way, k - 1 if way == 0 else k).wait_recv()
        for p in range(2):
            mine = chunk(z + 8 - 2 * k if way == 0 else z - 6 + 2 * k, p)
            if not first:
                leaf = leaf_in(way, k - 1 if way == 0 else k)
                mine += half(leaf, p)[...].astype(jnp.float32)
            if k > 0:
                rs_chain(way, k - 1, p).wait_recv()
                mine += half(chain_in(way, k - 1), p)[...].astype(jnp.float32)
            half(chain_source(way, k), p)[...] = mine.astype(jnp.bfloat16)
            rs_chain(way, k, p).start()

    def to_partner():
        return remote(shards.at[1 - ylo], other, o_s, o_r, partner)

    def turn(h, ref, xx):
        piece = jnp.concatenate([ref[0, xx], ref[1, xx]], axis=0)
        lrow[h, :, pl.ds(xx * 2 * SHARD, 2 * SHARD)] = piece.T

    send_chain(0, 0)
    send_leaf(1, 0)
    send_leaf(0, 0)
    send_leaf(1, 1)
    to_partner().start()
    turn(ylo, shards.at[ylo], 0)
    for k in range(3):
        send_chain(1, k)
        send_chain(0, k + 1)
        send_leaf(0, k + 1)
        if k < 2:
            send_leaf(1, k + 2)
        turn(ylo, shards.at[ylo], k + 1)

    loads[2].wait()
    own = chunk(z)
    for way in range(2):
        rs_leaf(way, 3).wait_recv()
        own += leaf_in(way, 3)[...].astype(jnp.float32)
    for way in (1, 0):
        for p in range(2):
            rs_chain(way, 3 - way, p).wait_recv()
        own += chain_in(way, 3 - way)[...].astype(jnp.float32)
    high, low = split_bf16(own)
    both = dot(jnp.concatenate([high, low], axis=0), whi[...], 1, 0)
    rotated = both[:OWN] + both[OWN:] + dot(high, wlo[...], 1, 0)
    moved = second_decay * mom[...] + (1.0 - second_decay) * rotated * rotated
    new_moments[...] = moved
    scaled = (rotated / jnp.sqrt(moved + moment_eps)).astype(jnp.bfloat16)
    back = dot(scaled, whi[...], 1, 1) + dot(scaled, wlo[...], 1, 1)
    gathered[ylo, z] = back.astype(jnp.bfloat16)

    def origin(way, o):
        return gathered.at[ylo, (z + Z - o) % Z if way == 0 else (z + o) % Z]

    def ag_chain(way, k, p, back=0):
        ref = half(origin(way, 2 * k + back), p)
        return remote(ref, ref, ag_s, ac_r.at[way, k, p], far[way])

    def ag_leaf(way, k, back=0):
        ref = origin(way, 2 * k + back)
        return remote(ref, ref, ag_s, al_r.at[way, k], near[way])

    def forward(way, o):
        ref = origin(way, o)
        remote(ref, ref, y_s, y_r, partner).start()

    for k in range(5):
        for way in range(2):
            last = 3 - way
            if k <= last + 1:
                for p in range(2):
                    if k > 0:
                        ag_chain(way, k - 1, p, 2).wait_recv()
                    if k <= last:
                        ag_chain(way, k, p).start()
                if k < 4:
                    ag_leaf(way, k).start()
        if k == 0:
            forward(0, 0)
        else:
            for way in range(2):
                if k <= 4 - way:
                    forward(way, 2 * k)
            for way in range(2):
                ag_leaf(way, k - 1, 1).wait_recv()
                forward(way, 2 * k - 1)
        if k == 0:
            to_partner().wait_recv()
        if k < 4:
            turn(1 - ylo, other, k)

    for lo, n in SPANS:
        total[:, pl.ds(lo, n)] = dot(lrow[ylo], gathered[ylo, :, :, pl.ds(lo, n)].reshape(HALF, n), 1, 0)
    whole = gathered.at[1 - ylo]
    remote(whole, whole, y_s, y_r, partner).wait_recv()
    for lo, n in SPANS:
        rest = dot(lrow[1 - ylo], gathered[1 - ylo, :, :, pl.ds(lo, n)].reshape(HALF, n), 1, 0)
        update[:, pl.ds(lo, n)] = (total[:, pl.ds(lo, n)] + rest).astype(jnp.bfloat16)

    pl.when(at_home)(to_across.wait_send)
    pl.when(away)(to_mate.wait_send)
    pl.when(away)(to_diagonal.wait_send)
    for r in range(2):
        for d in range(1, X):
            to_x(r, d).wait_send()
        to_core(r).wait_send()
    to_partner().wait_send()
    remote(rows.at[ylo], rows.at[ylo], g_s, g_r, partner).wait_send()
    remote(slots, slots, rs_s, o_r, partner).wait_send()
    sent = gathered.at[ylo, pl.ds(0, Z - 1)]
    remote(sent, sent, ag_s, o_r, partner).wait_send()
    remote(whole, whole, y_s, y_r, partner).wait_send()


def per_device(grad, left_basis, right_basis, moments):
    bf16, f32 = jnp.bfloat16, jnp.float32
    dma = pltpu.SemaphoreType.DMA
    vmem = pl.BlockSpec(memory_space=pltpu.VMEM)
    hbm = pl.BlockSpec(memory_space=pl.ANY)
    scratch = [
        pltpu.VMEM((2, 2, X, SHARD, ROWS), bf16),
        pltpu.VMEM((2, X, SHARD, ROWS), bf16),
        pltpu.VMEM((2, ROWS, HALF), bf16),
        pltpu.VMEM((2, ROWS, COLS), bf16),
        pltpu.VMEM((COLS, COLS), f32),
        pltpu.VMEM((COLS, COLS), bf16),
        pltpu.VMEM((COLS, COLS), bf16),
        pltpu.VMEM((OWN, COLS), f32),
        pltpu.VMEM((HALF, COLS), f32),
        pltpu.VMEM((9, OWN, COLS), bf16),
        pltpu.VMEM((15, OWN, COLS), bf16),
        pltpu.VMEM((2, Z, OWN, COLS), bf16),
        pltpu.VMEM((ROWS, COLS), f32),
    ]
    scratch += [dma((4,)), dma((2,)), dma((2,)), dma((2, 3)), dma((2, 3)), dma((2,)), dma((2,)), dma, dma, dma, dma]
    scratch += [dma, dma((2, 4, 2)), dma((2, 4)), dma, dma((2, 4, 2)), dma((2, 4)), dma, dma]
    return pl.pallas_call(
        kernel,
        out_shape=(
            jax.ShapeDtypeStruct((OWN, COLS), f32),
            jax.ShapeDtypeStruct((ROWS, COLS), bf16),
        ),
        in_specs=[hbm, hbm, hbm, hbm],
        out_specs=(vmem, vmem),
        scratch_shapes=scratch,
        compiler_params=pltpu.CompilerParams(
            collective_id=0, has_side_effects=True, vmem_limit_bytes=62 * 2**20
        ),
    )(grad, left_basis.T, right_basis, moments)


def solution(mesh):
    return jax.shard_map(
        per_device,
        mesh=mesh,
        in_specs=(P("dp", "tensor"), P("dp", "tensor"), P("tensor", None), P("dp", "tensor")),
        out_specs=(P("dp", "tensor"), P("dp", "tensor")),
        check_vma=False,
    )
```

time: 322 us -> 76.1 us (0.24)
  waiting for transfers between devices: 270 us -> 0 us
  Pallas kernels: 0 us -> 71.9 us
  blocking collectives: 22.3 us -> 0 us
  between operations: 14.1 us -> 0.64 us
  matrix products: 11.5 us -> 0 us
    reduce_scatter x1 -> x0, waiting for transfers between devices: 146 us -> none  [per_device(): lax.psum_scatter(lax.dot_general(left_rows, grad, (((0,), (0,)), ((), ())...]
    all_gather x1 -> x0, waiting for transfers between devices: 124 us -> none  [per_device(): gathered = lax.all_gather(unrotated, 'dp', axis=0, tiled=True)]
    pallas_call x0 -> x1, Pallas kernels: none -> 71.9 us  [per_device(): pl.pallas_call(kernel, out_shape=(jax.ShapeDtypeStruct((OWN, COLS), f32),...]
    all_gather x1 -> x0, blocking collectives: 22.3 us -> none  [per_device(): left_rows = lax.all_gather(left_basis, 'tensor', axis=1, tiled=True)]
    dot_general x4 -> x0, matrix products: 11.5 us -> none  [the longest x1 3.54 us: per_device(): lax.dot_general(left_rows, grad, (((0,), (0,)), ((), ())), preferred_elem...]
  transfers between devices with their start and end apart: 2 -> 0, of which waited for: 2 -> 0; matrix products, arithmetic and copies ran while one was open for 0% -> 0% of each run, Pallas kernels for 0% -> 0%
where the time goes in v3:
time: 76.1 us; the launch traced here: 75.9 us
  Pallas kernels  71.9 us (94%)
  local copies, waits for them, and re-layouts  3.37 us (4%)
    pallas_call x1, Pallas kernels, per_device(): pl.pallas_call(kernel, out_shape=(jax.ShapeDtypeStruct((OWN, COLS), f32),...  71.9 us
    unnamed x2, local copies, waits for them, and re-layouts  3.37 us

profile of v3, /device:TPU:6, one launch (start us, length us, event | category | flops | bytes accessed | tf_op | source)
XLA Modules:
  0.0 75.9 jit_solution(1499016310310860604)
XLA Ops:
  0.6 71.9 %shard_map.59 = (f32[32,896]{1,0:T(8,128)}, bf16[256,896]{1,0:T(8,128)(2,1)}) custom-call(bf16[256,896]{1,0:T(8,128)(2,1)} %grad.1, bf16[64,256]{1,0:T(8,128)(2,1)} %bitcast.1, f32[896,896]{1,0:T(8,128)} %right.1, f32[32,896]{1,0:T(8,128)} %moments.1), custom_call_target="tpu_custom_call" | custom-call | tf_op jit(solution)/shard_map/pallas_call | solution.py:311
  72.6 1.6 %copy.8 = f32[32,896]{1,0:T(8,128)} copy(f32[32,896]{1,0:T(8,128)} %get-tuple-element.4) | data formatting | bytes 229376
  74.1 1.8 %copy.9 = bf16[256,896]{1,0:T(8,128)(2,1)} copy(bf16[256,896]{1,0:T(8,128)(2,1)} %get-tuple-element.5) | data formatting | bytes 917504

commit v4 on v3

v4 whole, which is shorter than its diff:
```python
import jax
import jax.numpy as jnp
from jax import lax
from jax.experimental import pallas as pl
from jax.experimental.pallas import tpu as pltpu
from jax.sharding import PartitionSpec as P

second_decay = 0.95
moment_eps = 1e-08

MESH = pl.DeviceIdType.MESH
Z, X = 16, 4
ROWS, COLS, OWN, SHARD = 256, 896, 32, 64
HALF = Z * OWN
JS = 2 * X
SPANS = ((0, 256), (256, 256), (512, 256), (768, 128))
PART = OWN // 2
GPARTS = 4
GFIRST = 2


def split_bf16(values):
    high = values.astype(jnp.bfloat16)
    return high, (values - high.astype(jnp.float32)).astype(jnp.bfloat16)


def dot(a, b, ca, cb):
    return lax.dot_general(a, b, (((ca,), (cb,)), ((), ())), preferred_element_type=jnp.float32)


def kernel(grad, left, right, moments, new_moments, update, *scratch):
    (shards, other, lrow, rows, w32, whi, wlo, mom, proj, leaving, slots, gathered, total) = scratch[:13]
    (loc_s, l_s, l_r, lx_s, lx_r, lc_s, lc_r, g_s, g_r, o_s, o_r, od_s, od_r) = scratch[13:26]
    (rs_s, rc_r, rl_r, ag_s, ac_r, al_r, y_s, y_r) = scratch[26:]
    dp, t = lax.axis_index("dp"), lax.axis_index("tensor")
    ylo, z = dp // Z, dp % Z
    yhi, j = t // JS, t % JS
    x, core = j // 2, j % 2
    is0, is1 = core == 0, core == 1

    def along(step):
        return (ylo * Z + (z + Z + step) % Z, t)

    near, far = (along(1), along(-1)), (along(2), along(-2))
    partner = ((1 - ylo) * Z + z, t)
    across = (dp, (1 - yhi) * JS + j)
    diagonal = ((1 - ylo) * Z + z, (1 - yhi) * JS + j)
    sibling = (dp, yhi * JS + x * 2 + (1 - core))
    xs = [(dp, yhi * JS + ((x + d) % X) * 2 + core) for d in range(1, X)]

    def remote(src, dst, ssem, rsem, dev):
        return pltpu.make_async_remote_copy(
            src_ref=src, dst_ref=dst, send_sem=ssem, recv_sem=rsem, device_id=dev, device_id_type=MESH
        )

    barrier = pltpu.get_barrier_semaphore()
    everyone = [*near, *far, partner, across, diagonal, sibling] + xs
    for dev in everyone:
        pl.semaphore_signal(barrier, inc=1, device_id=dev, device_id_type=MESH)
    here = shards.at[ylo, core, x]
    loads = [
        pltpu.make_async_copy(grad, rows.at[ylo], loc_s.at[0]),
        pltpu.make_async_copy(right, w32, loc_s.at[1]),
        pltpu.make_async_copy(moments, mom, loc_s.at[2]),
    ]
    keep = pltpu.make_async_copy(left, here, loc_s.at[3])
    at_home = ylo == yhi
    away = jnp.logical_not(at_home)
    pl.when(at_home)(keep.start)
    for load in loads:
        load.start()
    pl.semaphore_wait(barrier, len(everyone))

    to_across = remote(left, here, l_s.at[0], l_r.at[ylo], across)
    to_mate = remote(left, here, l_s.at[0], l_r.at[ylo], partner)
    to_diagonal = remote(left, here, l_s.at[1], l_r.at[ylo], diagonal)
    pl.when(at_home)(to_across.start)
    pl.when(away)(to_mate.start)
    pl.when(away)(to_diagonal.start)

    def grad_part(p):
        cut = pl.ds(p * (ROWS // GPARTS), ROWS // GPARTS)
        return remote(grad.at[cut], rows.at[ylo, cut], g_s, g_r, partner)

    for p in range(GFIRST):
        grad_part(p).start()

    def to_x(r, d):
        ref = shards.at[r, core, x]
        return remote(ref, ref, lx_s.at[r, d - 1], lx_r.at[r, d - 1], xs[d - 1])

    def from_x(r, d):
        ref = shards.at[r, core, (x + X - d) % X]
        return remote(ref, ref, lx_s.at[r, d - 1], lx_r.at[r, d - 1], xs[d - 1])

    def to_core(r):
        ref = shards.at[r, core]
        return remote(ref, ref, lc_s.at[r], lc_r.at[r], sibling)

    def from_core(r):
        ref = shards.at[r, 1 - core]
        return remote(ref, ref, lc_s.at[r], lc_r.at[r], sibling)

    for k in range(2):
        r = (ylo + k) % 2
        arrived = remote(left, shards.at[r, core, x], l_s.at[0], l_r.at[r], sibling).wait_recv
        if k == 0:
            pl.when(at_home)(keep.wait)
            pl.when(away)(arrived)
        else:
            arrived()
        for d in range(1, X):
            to_x(r, d).start()

    for p in range(GFIRST, GPARTS):
        grad_part(p).start()
    loads[1].wait()
    for lo in range(0, COLS, 128):
        high, low = split_bf16(w32[pl.ds(lo, 128), :])
        whi[pl.ds(lo, 128), :] = high
        wlo[pl.ds(lo, 128), :] = low

    for k in range(2):
        r = (ylo + k) % 2
        for d in range(1, X):
            from_x(r, d).wait_recv()
        to_core(r).start()

    loads[0].wait()
    remote(grad, rows.at[1 - ylo], g_s, g_r, partner).wait_recv()
    for r in range(2):
        from_core(r).wait_recv()

    def project(p):
        for lo, n in SPANS:
            part = sum(
                dot(shards[r, :, :, :, p].reshape(HALF // 2, ROWS), rows[r, :, pl.ds(lo, n)], 1, 0) for r in range(2)
            )
            proj[p, :, :, pl.ds(lo, n)] = part.reshape(Z, PART, n)

    def chunk(d, p):
        d = (d + Z) % Z
        return proj[p, ((d // 2) % 2) * JS + (d // 4) * 2 + d % 2]

    def chain_in(way, k, p):
        return slots.at[4 * way + k, p]

    def leaf_in(way, k, p):
        return slots.at[7 + 4 * way + k, p]

    def chain_source(way, k, p):
        if way == 0:
            return leaving.at[0, p] if k == 0 else chain_in(0, k - 1, p)
        return leaf_in(1, k, p)

    def rs_chain(way, k, p):
        return remote(chain_source(way, k, p), chain_in(way, k, p), rs_s, rc_r.at[way, k, p], far[way])

    def rs_leaf(way, k, p):
        return remote(leaving.at[1 + 4 * way + k, p], leaf_in(way, k, p), rs_s, rl_r.at[way, k, p], near[way])

    def send_leaf(way, k, p):
        leaving[1 + 4 * way + k, p] = chunk(z + 7 - 2 * k if way == 0 else z - 7 + 2 * k, p).astype(jnp.bfloat16)
        rs_leaf(way, k, p).start()

    def send_chain(way, k, p):
        mine = chunk(z + 8 - 2 * k if way == 0 else z - 6 + 2 * k, p)
        leaf = k - 1 if way == 0 else k
        if leaf >= 0:
            rs_leaf(way, leaf, p).wait_recv()
            mine += leaf_in(way, leaf, p)[...].astype(jnp.float32)
        if k > 0:
            rs_chain(way, k - 1, p).wait_recv()
            mine += chain_in(way, k - 1, p)[...].astype(jnp.float32)
        chain_source(way, k, p)[...] = mine.astype(jnp.bfloat16)
        rs_chain(way, k, p).start()

    def sum_step(k, p):
        if k > 0:
            send_chain(1, k - 1, p)
        send_chain(0, k, p)
        if k == 0:
            send_leaf(1, 0, p)
        send_leaf(0, k, p)
        if k < 3:
            send_leaf(1, k + 1, p)

    def to_partner(c, xx):
        return remote(shards.at[1 - ylo, c, xx], other.at[c, xx], o_s, o_r, partner)

    def all_from_partner():
        return remote(other, other, o_s, o_r, partner)

    def across_cores():
        return remote(other, other, od_s, od_r, sibling)

    def turn(h, ref, xx):
        piece = jnp.concatenate([ref[c, xx].reshape(SHARD, ROWS) for c in range(2)], axis=0)
        lrow[h, :, pl.ds(xx * 2 * SHARD, 2 * SHARD)] = piece.T

    for p in range(2):
        project(p)
        sum_step(0, p)
    for k in range(1, 4):

        @pl.when(is1)
        def _():
            for xx in range(X):
                if xx == k or (xx, k) == (0, 1):
                    for c in range(2):
                        to_partner(c, xx).start()

        turn(ylo, shards.at[ylo], k - 1)
        for p in range(2):
            sum_step(k, p)
    turn(ylo, shards.at[ylo], 3)

    def own_step(p):
        own = chunk(z, p)
        for way in range(2):
            rs_leaf(way, 3, p).wait_recv()
            own += leaf_in(way, 3, p)[...].astype(jnp.float32)
        for way in (1, 0):
            rs_chain(way, 3 - way, p).wait_recv()
            own += chain_in(way, 3 - way, p)[...].astype(jnp.float32)
        high, low = split_bf16(own)
        both = dot(jnp.concatenate([high, low], axis=0), whi[...], 1, 0)
        rotated = both[:PART] + both[PART:] + dot(high, wlo[...], 1, 0)
        moved = second_decay * mom[pl.ds(p * PART, PART), :] + (1.0 - second_decay) * rotated * rotated
        new_moments[pl.ds(p * PART, PART), :] = moved
        scaled = (rotated / jnp.sqrt(moved + moment_eps)).astype(jnp.bfloat16)
        back = dot(scaled, whi[...], 1, 1) + dot(scaled, wlo[...], 1, 1)
        gathered[ylo, z, p] = back.astype(jnp.bfloat16)

    def origin(way, o, p):
        return gathered.at[ylo, (z + Z - o) % Z if way == 0 else (z + o) % Z, p]

    def ag_chain(way, k, p, back=0):
        ref = origin(way, 2 * k + back, p)
        return remote(ref, ref, ag_s, ac_r.at[way, k, p], far[way])

    def ag_leaf(way, k, p, back=0):
        ref = origin(way, 2 * k + back, p)
        return remote(ref, ref, ag_s, al_r.at[way, k, p], near[way])

    def forward(way, o, p):
        ref = origin(way, o, p)
        remote(ref, ref, y_s, y_r, partner).start()

    def gather_step(k, p):
        for way in range(2):
            last = 3 - way
            if 0 < k <= last + 1:
                ag_chain(way, k - 1, p, 2).wait_recv()
            if k <= last:
                ag_chain(way, k, p).start()
        for way in range(2):
            if k < 4:
                ag_leaf(way, k, p).start()
        if k == 0:
            forward(0, 0, p)
        else:
            for way in range(2):
                if k <= 4 - way:
                    forward(way, 2 * k, p)
            for way in range(2):
                ag_leaf(way, k - 1, p, 1).wait_recv()
                forward(way, 2 * k - 1, p)

    loads[2].wait()
    for p in range(2):
        own_step(p)
        gather_step(0, p)

    @pl.when(is1)
    def _():
        all_from_partner().wait_recv()
        across_cores().start()

    for k in range(1, 5):
        for p in range(2):
            gather_step(k, p)
        if k == 1:
            pl.when(is0)(across_cores().wait_recv)
        elif k < 4:
            for xx in range(2 * k - 4, 2 * k - 2):
                turn(1 - ylo, other, xx)

    for lo, n in SPANS:
        total[:, pl.ds(lo, n)] = dot(lrow[ylo], gathered[ylo, :, :, :, pl.ds(lo, n)].reshape(HALF, n), 1, 0)
    whole = gathered.at[1 - ylo]
    remote(whole, whole, y_s, y_r, partner).wait_recv()
    for lo, n in SPANS:
        rest = dot(lrow[1 - ylo], gathered[1 - ylo, :, :, :, pl.ds(lo, n)].reshape(HALF, n), 1, 0)
        update[:, pl.ds(lo, n)] = (total[:, pl.ds(lo, n)] + rest).astype(jnp.bfloat16)

    pl.when(at_home)(to_across.wait_send)
    pl.when(away)(to_mate.wait_send)
    pl.when(away)(to_diagonal.wait_send)
    for r in range(2):
        for d in range(1, X):
            to_x(r, d).wait_send()
        to_core(r).wait_send()
    pl.when(is1)(all_from_partner().wait_send)
    pl.when(is1)(across_cores().wait_send)
    remote(rows.at[ylo], rows.at[ylo], g_s, g_r, partner).wait_send()
    remote(slots, slots, rs_s, o_r, partner).wait_send()
    sent = gathered.at[ylo, pl.ds(0, Z - 1)]
    remote(sent, sent, ag_s, o_r, partner).wait_send()
    remote(whole, whole, y_s, y_r, partner).wait_send()


def per_device(grad, left_basis, right_basis, moments):
    bf16, f32 = jnp.bfloat16, jnp.float32
    dma = pltpu.SemaphoreType.DMA
    vmem = pl.BlockSpec(memory_space=pltpu.VMEM)
    hbm = pl.BlockSpec(memory_space=pl.ANY)
    scratch = [
        pltpu.VMEM((2, 2, X, 2, 2, PART, ROWS), bf16),
        pltpu.VMEM((2, X, 2, 2, PART, ROWS), bf16),
        pltpu.VMEM((2, ROWS, HALF), bf16),
        pltpu.VMEM((2, ROWS, COLS), bf16),
        pltpu.VMEM((COLS, COLS), f32),
        pltpu.VMEM((COLS, COLS), bf16),
        pltpu.VMEM((COLS, COLS), bf16),
        pltpu.VMEM((OWN, COLS), f32),
        pltpu.VMEM((2, Z, PART, COLS), f32),
        pltpu.VMEM((9, 2, PART, COLS), bf16),
        pltpu.VMEM((15, 2, PART, COLS), bf16),
        pltpu.VMEM((2, Z, 2, PART, COLS), bf16),
        pltpu.VMEM((ROWS, COLS), f32),
    ]
    scratch += [dma((4,)), dma((2,)), dma((2,)), dma((2, 3)), dma((2, 3)), dma((2,)), dma((2,)), dma, dma, dma, dma, dma, dma]
    scratch += [dma, dma((2, 4, 2)), dma((2, 4, 2)), dma, dma((2, 4, 2)), dma((2, 4, 2)), dma, dma]
    return pl.pallas_call(
        kernel,
        out_shape=(pltpu.VMEM((OWN, COLS), f32), pltpu.VMEM((ROWS, COLS), bf16)),
        in_specs=[hbm, hbm, hbm, hbm],
        out_specs=(vmem, vmem),
        scratch_shapes=scratch,
        compiler_params=pltpu.CompilerParams(
            collective_id=0, has_side_effects=True, vmem_limit_bytes=62 * 2**20
        ),
    )(grad, left_basis.T.reshape(2, 2, PART, ROWS), right_basis, moments)


def solution(mesh):
    return jax.shard_map(
        per_device,
        mesh=mesh,
        in_specs=(P("dp", "tensor"), P("dp", "tensor"), P("tensor", None), P("dp", "tensor")),
        out_specs=(P("dp", "tensor"), P("dp", "tensor")),
        check_vma=False,
    )
```

time: 76.1 us -> 68.3 us (0.90)
  Pallas kernels: 71.9 us -> 65.6 us
  local copies, waits for them, and re-layouts: 3.37 us -> 1.42 us
    pallas_call x1, Pallas kernels: 71.9 us -> 65.6 us  [per_device(): pl.pallas_call(kernel, out_shape=(pltpu.VMEM((OWN, COLS), f32), pltpu.VME...]
    unnamed x2, local copies, waits for them, and re-layouts: 3.37 us -> 1.42 us
where the time goes in v4:
time: 68.3 us; the launch traced here: 67.7 us
  Pallas kernels  65.6 us (96%)
  local copies, waits for them, and re-layouts  1.42 us (2%)
    pallas_call x1, Pallas kernels, per_device(): pl.pallas_call(kernel, out_shape=(pltpu.VMEM((OWN, COLS), f32), pltpu.VME...  65.6 us
    unnamed x2, local copies, waits for them, and re-layouts  1.42 us

profile of v4, /device:TPU:6, one launch (start us, length us, event | category | flops | bytes accessed | tf_op | source)
XLA Modules:
  0.0 67.7 jit_solution(17042358718005127857)
XLA Ops:
  0.6 65.6 %shard_map.59 = (f32[32,896]{1,0:T(8,128)S(1)}, bf16[256,896]{1,0:T(8,128)(2,1)S(1)}) custom-call(bf16[256,896]{1,0:T(8,128)(2,1)} %grad.1, bf16[2,2,16,256]{3,2,1,0:T(8,128)(2,1)} %bitcast.3, f32[896,896]{1,0:T(8,128)} %right.1, f32[32,896]{1,0:T(8,128)} %moments.1), custom_call_target="tpu_custom_call" | custom-call | tf_op jit(solution)/shard_map/pallas_call | solution.py:335
  66.3 0.6 copy.8
  66.9 0.8 %copy.9 = bf16[256,896]{1,0:T(8,128)(2,1)} copy(bf16[256,896]{1,0:T(8,128)(2,1)S(1)} %get-tuple-element.3) | data formatting | bytes 917504

commit v5 on v4

--- a/solution.py
+++ b/solution.py
@@ -15,7 +15,7 @@
 JS = 2 * X
 SPANS = ((0, 256), (256, 256), (512, 256), (768, 128))
 PART = OWN // 2
-GPARTS = 4
+GPARTS = len(SPANS)
 GFIRST = 2
 
 
@@ -29,9 +29,9 @@
 
 
 def kernel(grad, left, right, moments, new_moments, update, *scratch):
-    (shards, other, lrow, rows, w32, whi, wlo, mom, proj, leaving, slots, gathered, total) = scratch[:13]
-    (loc_s, l_s, l_r, lx_s, lx_r, lc_s, lc_r, g_s, g_r, o_s, o_r, od_s, od_r) = scratch[13:26]
-    (rs_s, rc_r, rl_r, ag_s, ac_r, al_r, y_s, y_r) = scratch[26:]
+    (shards, other, lrow, rows, w32, whi, wlo, mom, proj, leaving, slots, gathered, total, thi) = scratch[:14]
+    (loc_s, l_s, l_r, lx_s, lx_r, lc_s, lc_r, g_s, g_r, o_s, o_r, od_s, od_r) = scratch[14:27]
+    (rs_s, rc_r, rl_r, ag_s, ac_r, al_r, y_s, y_r, row_ok, yk_r, a2_s, a2_r) = scratch[27:]
     dp, t = lax.axis_index("dp"), lax.axis_index("tensor")
     ylo, z = dp // Z, dp % Z
     yhi, j = t // JS, t % JS
@@ -42,6 +42,10 @@
         return (ylo * Z + (z + Z + step) % Z, t)
 
     near, far = (along(1), along(-1)), (along(2), along(-2))
+
+    def beside(step):
+        return ((1 - ylo) * Z + (z + Z + step) % Z, t)
+
     partner = ((1 - ylo) * Z + z, t)
     across = (dp, (1 - yhi) * JS + j)
     diagonal = ((1 - ylo) * Z + z, (1 - yhi) * JS + j)
@@ -70,6 +74,7 @@
     for load in loads:
         load.start()
     pl.semaphore_wait(barrier, len(everyone))
+    pl.semaphore_signal(row_ok, inc=1, device_id=partner, device_id_type=MESH)
 
     to_across = remote(left, here, l_s.at[0], l_r.at[ylo], across)
     to_mate = remote(left, here, l_s.at[0], l_r.at[ylo], partner)
@@ -79,8 +84,9 @@
     pl.when(away)(to_diagonal.start)
 
     def grad_part(p):
-        cut = pl.ds(p * (ROWS // GPARTS), ROWS // GPARTS)
-        return remote(grad.at[cut], rows.at[ylo, cut], g_s, g_r, partner)
+        lo, n = SPANS[p]
+        cut = rows.at[ylo, :, pl.ds(lo, n)]
+        return remote(grad.at[:, pl.ds(lo, n)], cut, g_s, g_r.at[p], partner)
 
     for p in range(GFIRST):
         grad_part(p).start()
@@ -119,6 +125,7 @@
         high, low = split_bf16(w32[pl.ds(lo, 128), :])
         whi[pl.ds(lo, 128), :] = high
         wlo[pl.ds(lo, 128), :] = low
+        thi[:, pl.ds(lo, 128)] = high.T
 
     for k in range(2):
         r = (ylo + k) % 2
@@ -127,16 +134,22 @@
         to_core(r).start()
 
     loads[0].wait()
-    remote(grad, rows.at[1 - ylo], g_s, g_r, partner).wait_recv()
     for r in range(2):
         from_core(r).wait_recv()
 
+    def term(r, p, lo, n):
+        part = dot(shards[r, :, :, :, p].reshape(HALF // 2, ROWS), rows[r, :, pl.ds(lo, n)], 1, 0)
+        return part.reshape(Z, PART, n)
+
+    for p in range(2):
+        for lo, n in SPANS:
+            proj[p, :, :, pl.ds(lo, n)] = term(ylo, p, lo, n)
+
     def project(p):
-        for lo, n in SPANS:
-            part = sum(
-                dot(shards[r, :, :, :, p].reshape(HALF // 2, ROWS), rows[r, :, pl.ds(lo, n)], 1, 0) for r in range(2)
-            )
-            proj[p, :, :, pl.ds(lo, n)] = part.reshape(Z, PART, n)
+        for i, (lo, n) in enumerate(SPANS):
+            if p == 0:
+                grad_part(i).wait_recv()
+            proj[p, :, :, pl.ds(lo, n)] += term(1 - ylo, p, lo, n)
 
     def chunk(d, p):
         d = (d + Z) % Z
@@ -229,8 +242,7 @@
         moved = second_decay * mom[pl.ds(p * PART, PART), :] + (1.0 - second_decay) * rotated * rotated
         new_moments[pl.ds(p * PART, PART), :] = moved
         scaled = (rotated / jnp.sqrt(moved + moment_eps)).astype(jnp.bfloat16)
-        back = dot(scaled, whi[...], 1, 1) + dot(scaled, wlo[...], 1, 1)
-        gathered[ylo, z, p] = back.astype(jnp.bfloat16)
+        gathered[ylo, z, p] = dot(scaled, thi[...], 1, 0).astype(jnp.bfloat16)
 
     def origin(way, o, p):
         return gathered.at[ylo, (z + Z - o) % Z if way == 0 else (z + o) % Z, p]
@@ -243,9 +255,21 @@
         ref = origin(way, 2 * k + back, p)
         return remote(ref, ref, ag_s, al_r.at[way, k, p], near[way])
 
-    def forward(way, o, p):
+    def forward(way, o, p, dev=partner, arrives=None):
         ref = origin(way, o, p)
-        remote(ref, ref, y_s, y_r, partner).start()
+        remote(ref, ref, y_s, y_r if arrives is None else arrives, dev).start()
+
+    def other_from(o, p):
+        return gathered.at[1 - ylo, (z + o) % Z, p]
+
+    def pass_other(k, p):
+        ref = other_from(2 * k, p)
+        remote(ref, ref, y_s, yk_r.at[k, p], partner).wait_recv()
+        remote(ref, ref, a2_s, a2_r.at[k, p], near[1]).start()
+
+    def other_passed(k, p):
+        ref = other_from(2 * k + 1, p)
+        remote(ref, ref, a2_s, a2_r.at[k, p], near[1]).wait_recv()
 
     def gather_step(k, p):
         for way in range(2):
@@ -257,15 +281,24 @@
         for way in range(2):
             if k < 4:
                 ag_leaf(way, k, p).start()
+        if k == 3:
+            if p == 0:
+                pl.semaphore_wait(row_ok, 1)
+            forward(0, 6, p, beside(2))
+            forward(0, 6, p, beside(1))
+            forward(1, 6, p, beside(-1))
         if k == 0:
-            forward(0, 0, p)
-        else:
-            for way in range(2):
-                if k <= 4 - way:
-                    forward(way, 2 * k, p)
+            forward(0, 0, p, arrives=yk_r.at[0, p])
+        elif k == 4:
             for way in range(2):
                 ag_leaf(way, k - 1, p, 1).wait_recv()
-                forward(way, 2 * k - 1, p)
+        else:
+            forward(0, 2 * k, p)
+            forward(1, 2 * k, p, arrives=yk_r.at[k, p] if k < 3 else None)
+            for way in range(2):
+                ag_leaf(way, k - 1, p, 1).wait_recv()
+            forward(0, 2 * k - 1, p)
+            pass_other(k - 1, p)
 
     loads[2].wait()
     for p in range(2):
@@ -288,8 +321,11 @@
 
     for lo, n in SPANS:
         total[:, pl.ds(lo, n)] = dot(lrow[ylo], gathered[ylo, :, :, :, pl.ds(lo, n)].reshape(HALF, n), 1, 0)
-    whole = gathered.at[1 - ylo]
-    remote(whole, whole, y_s, y_r, partner).wait_recv()
+    most = gathered.at[1 - ylo, pl.ds(0, 10)]
+    remote(most, most, y_s, y_r, partner).wait_recv()
+    for k in range(3):
+        for p in range(2):
+            other_passed(k, p)
     for lo, n in SPANS:
         rest = dot(lrow[1 - ylo], gathered[1 - ylo, :, :, :, pl.ds(lo, n)].reshape(HALF, n), 1, 0)
         update[:, pl.ds(lo, n)] = (total[:, pl.ds(lo, n)] + rest).astype(jnp.bfloat16)
@@ -307,7 +343,10 @@
     remote(slots, slots, rs_s, o_r, partner).wait_send()
     sent = gathered.at[ylo, pl.ds(0, Z - 1)]
     remote(sent, sent, ag_s, o_r, partner).wait_send()
-    remote(whole, whole, y_s, y_r, partner).wait_send()
+    sent = gathered.at[1 - ylo, pl.ds(0, 13)]
+    remote(sent, sent, y_s, y_r, partner).wait_send()
+    sent = gathered.at[1 - ylo, pl.ds(0, 3)]
+    remote(sent, sent, a2_s, y_r, partner).wait_send()
 
 
 def per_device(grad, left_basis, right_basis, moments):
@@ -329,9 +368,11 @@
         pltpu.VMEM((15, 2, PART, COLS), bf16),
         pltpu.VMEM((2, Z, 2, PART, COLS), bf16),
         pltpu.VMEM((ROWS, COLS), f32),
+        pltpu.VMEM((COLS, COLS), bf16),
     ]
-    scratch += [dma((4,)), dma((2,)), dma((2,)), dma((2, 3)), dma((2, 3)), dma((2,)), dma((2,)), dma, dma, dma, dma, dma, dma]
-    scratch += [dma, dma((2, 4, 2)), dma((2, 4, 2)), dma, dma((2, 4, 2)), dma((2, 4, 2)), dma, dma]
+    scratch += [dma((4,)), dma((2,)), dma((2,)), dma((2, 3)), dma((2, 3)), dma((2,)), dma((2,)), dma, dma((GPARTS,)), dma, dma, dma, dma]
+    scratch += [dma, dma((2, 4, 2)), dma((2, 4, 2)), dma, dma((2, 4, 2)), dma((2, 4, 2)), dma, dma, pltpu.SemaphoreType.REGULAR]
+    scratch += [dma((3, 2)), dma, dma((3, 2))]
     return pl.pallas_call(
         kernel,
         out_shape=(pltpu.VMEM((OWN, COLS), f32), pltpu.VMEM((ROWS, COLS), bf16)),

time: 68.3 us -> 66.7 us (0.977)
  Pallas kernels: 65.6 us -> 64.1 us
    pallas_call x1, Pallas kernels: 65.6 us -> 64.1 us  [per_device(): pl.pallas_call(kernel, out_shape=(pltpu.VMEM((OWN, COLS), f32), pltpu.VME...]
where the time goes in v5:
time: 66.7 us; the launch traced here: 66.2 us
  Pallas kernels  64.1 us (96%)
  local copies, waits for them, and re-layouts  1.42 us (2%)
    pallas_call x1, Pallas kernels, per_device(): pl.pallas_call(kernel, out_shape=(pltpu.VMEM((OWN, COLS), f32), pltpu.VME...  64.1 us
    unnamed x2, local copies, waits for them, and re-layouts  1.42 us

profile of v5, /device:TPU:6, one launch (start us, length us, event | category | flops | bytes accessed | tf_op | source)
XLA Modules:
  0.0 66.2 jit_solution(1952627589377865618)
XLA Ops:
  0.6 64.1 %shard_map.59 = (f32[32,896]{1,0:T(8,128)S(1)}, bf16[256,896]{1,0:T(8,128)(2,1)S(1)}) custom-call(bf16[256,896]{1,0:T(8,128)(2,1)} %grad.1, bf16[2,2,16,256]{3,2,1,0:T(8,128)(2,1)} %bitcast.3, f32[896,896]{1,0:T(8,128)} %right.1, f32[32,896]{1,0:T(8,128)} %moments.1), custom_call_target="tpu_custom_call" | custom-call | tf_op jit(solution)/shard_map/pallas_call | solution.py:376
  64.7 0.6 copy.8
  65.4 0.8 %copy.9 = bf16[256,896]{1,0:T(8,128)(2,1)} copy(bf16[256,896]{1,0:T(8,128)(2,1)S(1)} %get-tuple-element.3) | data formatting | bytes 917504

commit v6 on v5

--- a/solution.py
+++ b/solution.py
@@ -13,10 +13,10 @@
 ROWS, COLS, OWN, SHARD = 256, 896, 32, 64
 HALF = Z * OWN
 JS = 2 * X
-SPANS = ((0, 256), (256, 256), (512, 256), (768, 128))
+SPANS = ((0, 512), (512, 384))
 PART = OWN // 2
 GPARTS = len(SPANS)
-GFIRST = 2
+GFIRST = 1
 
 
 def split_bf16(values):
@@ -215,6 +215,8 @@
         project(p)
         sum_step(0, p)
     for k in range(1, 4):
+        for p in range(2):
+            sum_step(k, p)
 
         @pl.when(is1)
         def _():
@@ -224,8 +226,6 @@
                         to_partner(c, xx).start()
 
         turn(ylo, shards.at[ylo], k - 1)
-        for p in range(2):
-            sum_step(k, p)
     turn(ylo, shards.at[ylo], 3)
 
     def own_step(p):

time: 66.7 us -> 66.9 us (level)
  no operation moved by 1% of the time
where the time goes in v6:
time: 66.9 us; the launch traced here: 66.8 us
  Pallas kernels  64.7 us (97%)
  local copies, waits for them, and re-layouts  1.42 us (2%)
    pallas_call x1, Pallas kernels, per_device(): pl.pallas_call(kernel, out_shape=(pltpu.VMEM((OWN, COLS), f32), pltpu.VME...  64.7 us
    unnamed x2, local copies, waits for them, and re-layouts  1.42 us

profile of v6, /device:TPU:6, one launch (start us, length us, event | category | flops | bytes accessed | tf_op | source)
XLA Modules:
  0.0 66.8 jit_solution(7953814580299497548)
XLA Ops:
  0.6 64.7 %shard_map.59 = (f32[32,896]{1,0:T(8,128)S(1)}, bf16[256,896]{1,0:T(8,128)(2,1)S(1)}) custom-call(bf16[256,896]{1,0:T(8,128)(2,1)} %grad.1, bf16[2,2,16,256]{3,2,1,0:T(8,128)(2,1)} %bitcast.3, f32[896,896]{1,0:T(8,128)} %right.1, f32[32,896]{1,0:T(8,128)} %moments.1), custom_call_target="tpu_custom_call" | custom-call | tf_op jit(solution)/shard_map/pallas_call | solution.py:376
  65.4 0.6 copy.8
  66.0 0.8 %copy.9 = bf16[256,896]{1,0:T(8,128)(2,1)} copy(bf16[256,896]{1,0:T(8,128)(2,1)S(1)} %get-tuple-element.3) | data formatting | bytes 917504

commit v7 on v6

--- a/solution.py
+++ b/solution.py
@@ -278,13 +278,14 @@
                 ag_chain(way, k - 1, p, 2).wait_recv()
             if k <= last:
                 ag_chain(way, k, p).start()
+        if k == 3:
+            if p == 0:
+                pl.semaphore_wait(row_ok, 1)
+            forward(0, 6, p, beside(2))
         for way in range(2):
             if k < 4:
                 ag_leaf(way, k, p).start()
         if k == 3:
-            if p == 0:
-                pl.semaphore_wait(row_ok, 1)
-            forward(0, 6, p, beside(2))
             forward(0, 6, p, beside(1))
             forward(1, 6, p, beside(-1))
         if k == 0:

time: 66.9 us -> 66.5 us (level)
  no operation moved by 1% of the time
where the time goes in v7:
time: 66.5 us; the launch traced here: 66.4 us
  Pallas kernels  64.3 us (97%)
  local copies, waits for them, and re-layouts  1.42 us (2%)
    pallas_call x1, Pallas kernels, per_device(): pl.pallas_call(kernel, out_shape=(pltpu.VMEM((OWN, COLS), f32), pltpu.VME...  64.3 us
    unnamed x2, local copies, waits for them, and re-layouts  1.42 us

profile of v7, /device:TPU:6, one launch (start us, length us, event | category | flops | bytes accessed | tf_op | source)
XLA Modules:
  0.0 66.4 jit_solution(1128589336139869277)
XLA Ops:
  0.6 64.3 %shard_map.59 = (f32[32,896]{1,0:T(8,128)S(1)}, bf16[256,896]{1,0:T(8,128)(2,1)S(1)}) custom-call(bf16[256,896]{1,0:T(8,128)(2,1)} %grad.1, bf16[2,2,16,256]{3,2,1,0:T(8,128)(2,1)} %bitcast.3, f32[896,896]{1,0:T(8,128)} %right.1, f32[32,896]{1,0:T(8,128)} %moments.1), custom_call_target="tpu_custom_call" | custom-call | tf_op jit(solution)/shard_map/pallas_call | solution.py:377
  64.9 0.6 copy.8
  65.6 0.8 %copy.9 = bf16[256,896]{1,0:T(8,128)(2,1)} copy(bf16[256,896]{1,0:T(8,128)(2,1)S(1)} %get-tuple-element.3) | data formatting | bytes 917504
